TPU v7x, 32 devices: a whole 2x2x4 slice. The times are simulated.
32 devices in a mesh: pix: 4 (over y, core), exp: 8 (over z, x).
Axes of the slice: x: 2, y: 2, z: 4, core: 2. Of those that a mesh axis runs over, the one named last changes fastest.
Arguments:
- design: bfloat16 [200, 196608], P(None, ('pix', 'exp')), may hold values from -1 to 1
- det_weight: float32 [196608], P(('pix', 'exp')), may hold values from 0.2 to 2
- outlier_mask: int32 [2, 196608], P(None, ('pix', 'exp')), may hold values from 0 to 1
- star_owner: int32 [196608, 1], P(('pix', 'exp')), may hold values from 0 to 31; in each aligned block of 6144 rows (0 to 6143, 6144 to 12287, ...) at most 384 rows name the same one
- star_slot: int32 [196608], P(('pix', 'exp')), may hold values from 0 to 767
- coef_init: float32 [64, 2, 200], P('exp'), may hold values from -6 to 6
- star_ref: float32 [2, 24576], P(None, ('pix', 'exp')), may hold values from -24 to 24
- star_prior: float32 [24576], P(('pix', 'exp')), may hold values from 0.2 to 2
Outputs:
- coefficients: float32 [64, 2, 200], P('exp')
- star_means: float32 [2, 24576], P(None, ('pix', 'exp'))
Inputs may be any that keep to these rules, and one draw needn't show every extreme that they name: `star_owner`: among the 6144 detections of one device, at most 384 name the same owner, and in every draw some device's detections name some owner exactly 384 times.
All inputs are finite; a program needn't handle non-finite values.
Results may differ from a plain program's by a relative error of at most 0.00045.
The roundings to bfloat16 on the way count: a program that leaves them out, or rounds other values in their place, can miss the bound.
Values sent between devices are 32-bit elements; how exact they have to be, the bound alone decides.
A program may use at most 64 MiB of HBM per device.

v0:
```python
import jax
import jax.numpy as jnp
from jax import lax
from jax.sharding import PartitionSpec as P

ITERS = 2


RIDGE = 0.5
STAR_BLOCKS = 8


def solve_blocks(gram_block, right_side):
    identity = jnp.eye(gram_block.shape[-1], dtype=jnp.float32)
    factor = jnp.linalg.cholesky(gram_block + RIDGE * identity)
    columns = jnp.swapaxes(right_side, 1, 2)
    middle = jax.scipy.linalg.solve_triangular(factor, columns, lower=True)
    update = jax.scipy.linalg.solve_triangular(factor, middle, lower=True, trans=1)
    return jnp.swapaxes(update, 1, 2)


def star_table(id_block, star_count):
    return (id_block[:, None] == jnp.arange(star_count, dtype=jnp.int32)[None, :]).astype(
        jnp.float32
    )


def on_device(
    design, det_weight, outlier_mask, star_owner, star_slot, coef_init, star_ref, star_prior
):
    highest = lax.Precision.HIGHEST
    peer_count = lax.axis_size(("pix", "exp"))
    pix_count = lax.axis_size("pix")
    term_count, row_count = design.shape
    maps_device = coef_init.shape[0]
    exp_rows_local = row_count // maps_device
    capacity = 2 * row_count // peer_count
    star_count = star_prior.shape[0]
    share_count = maps_device // pix_count
    slot_total = peer_count * capacity
    block_width = slot_total // STAR_BLOCKS
    owner_index = star_owner[:, 0]
    owner_hot = (owner_index[:, None] == jnp.arange(peer_count, dtype=jnp.int32)[None, :]).astype(
        jnp.float32
    )
    count_before = jnp.cumsum(owner_hot, axis=0) - owner_hot
    position = jnp.sum(count_before * owner_hot, axis=1).astype(jnp.int32)
    place_hot = (position[:, None] == jnp.arange(capacity, dtype=jnp.int32)[None, :]).astype(
        jnp.float32
    )

    def place(values):
        spread = values[:, :, None] * place_hot[None, :, :]
        placed = jnp.einsum("cip,io->cop", spread, owner_hot, precision=highest)
        return placed.reshape(values.shape[0], slot_total)

    id_buffer = place(star_slot.astype(jnp.float32)[None, :])[0].astype(jnp.int32)
    got_ids = lax.all_to_all(
        id_buffer.reshape(peer_count, capacity),
        ("pix", "exp"),
        split_axis=0,
        concat_axis=0,
        tiled=True,
    )
    id_blocks = got_ids.reshape(STAR_BLOCKS, block_width)
    design_blocks = design.reshape(term_count, maps_device, exp_rows_local)
    coefficients = coef_init
    star_means = jnp.zeros((2, star_count), jnp.float32)
    for step_index in range(ITERS):
        masked_weight = det_weight * outlier_mask[step_index].astype(jnp.float32)
        weighted = (
            (design * masked_weight[None, :])
            .astype(jnp.bfloat16)
            .reshape(term_count, maps_device, exp_rows_local)
        )
        gram_local = jnp.einsum(
            "tjr,ujr->jtu", weighted, design_blocks, preferred_element_type=jnp.float32
        )
        predicted = jnp.einsum(
            "jct,tjr->cjr",
            coefficients.astype(jnp.bfloat16),
            design_blocks,
            preferred_element_type=jnp.float32,
        ).reshape(2, row_count)
        payload = jnp.concatenate([predicted, masked_weight[None, :]], axis=0)
        forward_payload = place(payload)
        forward_delivered = lax.all_to_all(
            forward_payload.reshape(3, peer_count, capacity),
            ("pix", "exp"),
            split_axis=1,
            concat_axis=1,
            tiled=True,
        )
        arrived = forward_delivered.reshape(3, slot_total)
        totals_in = jnp.concatenate([arrived[2:] * arrived[:2], arrived[2:]], axis=0)
        value_blocks = jnp.swapaxes(totals_in.reshape(3, STAR_BLOCKS, block_width), 0, 1)

        def accumulate(pair):
            id_block, value_block = pair
            return jnp.dot(value_block, star_table(id_block, star_count), precision=highest)

        totals = jnp.sum(lax.map(accumulate, (id_blocks, value_blocks)), axis=0)
        star_means = (star_prior * star_ref + totals[:2]) / (star_prior + totals[2])

        def lookup(id_block):
            return jnp.dot(star_means, star_table(id_block, star_count).T, precision=highest)

        means_at_slots = jnp.swapaxes(lax.map(lookup, id_blocks), 0, 1).reshape(2, slot_total)
        delivered = lax.all_to_all(
            means_at_slots.reshape(2, peer_count, capacity),
            ("pix", "exp"),
            split_axis=1,
            concat_axis=1,
            tiled=True,
        )
        buffer = delivered.reshape(2, slot_total)
        shaped = buffer.reshape(buffer.shape[0], peer_count, capacity)
        pick_spread = jnp.einsum("cop,io->cip", shaped, owner_hot, precision=highest)
        returned = jnp.sum(pick_spread * place_hot[None, :, :], axis=2)
        residual_lo = (
            (returned - predicted).astype(jnp.bfloat16).reshape(2, maps_device, exp_rows_local)
        )
        right_side = jnp.einsum(
            "tjr,cjr->jct", weighted, residual_lo, preferred_element_type=jnp.float32
        )
        gram_part, right_part = (
            lax.psum_scatter(gram_local, "pix", scatter_dimension=0, tiled=True),
            lax.psum_scatter(right_side, "pix", scatter_dimension=0, tiled=True),
        )
        own_maps = lax.dynamic_slice_in_dim(
            coefficients, lax.axis_index("pix") * share_count, share_count, 0
        )
        coefficients = lax.all_gather(
            own_maps + solve_blocks(gram_part, right_part), "pix", axis=0, tiled=True
        )
    return (coefficients, star_means)


def solution(mesh):
    placed = (
        P(None, ("pix", "exp")),
        P(("pix", "exp")),
        P(None, ("pix", "exp")),
        P(("pix", "exp"), None),
        P(("pix", "exp")),
        P("exp", None, None),
        P(None, ("pix", "exp")),
        P(("pix", "exp")),
    )
    return jax.shard_map(
        on_device,
        mesh=mesh,
        in_specs=placed,
        out_specs=(P("exp", None, None), P(None, ("pix", "exp"))),
        check_vma=False,
    )
```

profile of v0, /device:TPU:0, one launch (start us, length us, event | category | flops | bytes accessed | tf_op | source)
XLA Modules:
  0.0 581.2 jit_solution(6260304657411567733)
XLA Ops:
  8.9 4.0 fusion.33
  17.5 16.7 %reduce-window.6 = f32[32,48,128]{2,1,0:T(8,128)S(1)} reduce-window(f32[32,48,128]{2,1,0:T(8,128)} %fusion.80, f32[]{:T(128)} %constant.141.clone.1), window={size=1x1x128 pad=0_0x0_0x127_0}, to_apply=%region_5.7 | reduce-window | flops 24969216 | bytes 1572868 | tf_op jit(solution)/shard_map/reduce-window
  35.6 5.6 fusion.69
  41.9 7.3 %all-to-all-start = ((s32[32,1,384]{2,1,0:T(1,128)}), s32[32,1,384]{2,1,0:T(1,128)S(1)}, u32[]{:S(2)}, u32[]{:S(2)}) async-start(s32[32,1,384]{2,1,0:T(1,128)} %copy.121), calls=%async_computation.1 | async-start | bytes 98304 | tf_op jit(solution)/shard_map/all_to_all | solution.py:58
  49.7 3.8 fusion.40
  53.5 4.8 fusion.32
  58.2 9.7 %copy.123 = f32[6144,384]{1,0:T(8,128)} copy(f32[6144,384]{0,1:T(8,128)} %fusion.32) | data formatting | bytes 18874368 | tf_op jit(solution)/shard_map/convert_element_type | solution.py:48
  68.5 14.4 %fusion.60 = f32[3,32,384]{2,1,0:T(8,128)S(1)} fusion(f32[6144,384]{1,0:T(8,128)} %copy.123, f32[3,6144]{1,0:T(4,128)S(1)} %pad_maximum_fusion.6, s32[6144]{0:T(1024)S(1)} %bitcast.241), kind=kOutput, calls=%fused_computation.73 | convolution fusion | flops 2725183488 | bytes 9682944 | tf_op jit(solution)/shard_map/cip,io->cop/dot_general | solution.py:54
  85.6 5.8 all-to-all-start.1
  92.8 7.1 %all-to-all-done.1 = f32[3,32,384]{2,0,1:T(4,128)S(1)} async-done(((f32[3,32,384]{2,0,1:T(4,128)}), f32[3,32,384]{2,0,1:T(4,128)S(1)}, u32[]{:S(2)}, u32[]{:S(2)}) %all-to-all-start.1) | async-done | bytes 147488 | tf_op jit(solution)/shard_map/all_to_all | solution.py:87
  100.4 13.3 %while.46 = (s32[]{:T(128)}, f32[8,3,768]{2,1,0:T(4,128)S(1)}, f32[8,3,1536]{2,1,0:T(4,128)S(1)}, s32[8,1536]{1,0:T(8,128)S(1)}, s32[]{:T(128)}) while((s32[]{:T(128)}, f32[8,3,768]{2,1,0:T(4,128)S(1)}, f32[8,3,1536]{2,1,0:T(4,128)S(1)}, s32[8,1536]{1,0:T(8,128)S(1)}, s32[]{:T(128)}) %tuple.113), condition=%wide.region_9.11_spmd, body=%wide.region_8.10_spmd.sunk | while | flops 43646976 | bytes 58433 | solution.py:102
  114.5 22.9 %while.47 = (s32[]{:T(128)}, f32[8,2,1536]{2,1,0:T(2,128)}, s32[8,1536]{1,0:T(8,128)S(1)}, f32[2,768]{1,0:T(2,128)S(1)}, s32[]{:T(128)}) while((s32[]{:T(128)}, f32[8,2,1536]{2,1,0:T(2,128)}, s32[8,1536]{1,0:T(8,128)S(1)}, f32[2,768]{1,0:T(2,128)S(1)}, s32[]{:T(128)}) %tuple.131), condition=%wide.region_12.14_spmd, body=%wide.region_11.13_spmd.sunk | while | flops 29491200 | bytes 37441 | solution.py:108
  114.5 2.8 fusion.154
  117.4 2.8 fusion.154
  120.3 2.8 fusion.154
  123.1 2.8 fusion.154
  128.8 2.8 fusion.154
  131.7 2.8 fusion.154
  134.6 2.8 fusion.154
  137.4 3.0 all-to-all-start.2
  141.1 6.9 %all-to-all-done.2 = f32[2,32,384]{2,0,1:T(2,128)S(1)} async-done(((f32[2,32,384]{2,0,1:T(2,128)}), f32[2,32,384]{2,0,1:T(2,128)S(1)}, u32[]{:S(2)}, u32[]{:S(2)}) %all-to-all-start.2) | async-done | bytes 98336 | tf_op jit(solution)/shard_map/all_to_all | solution.py:109
  148.0 10.6 %multiply_reduce_fusion.1 = f32[6144,2]{0,1:T(2,128)S(1)} fusion(f32[6144,384]{0,1:T(8,128)} %fusion.32, s32[6144]{0:T(1024)S(1)} %bitcast.242, f32[2,32,384]{2,0,1:T(2,128)S(1)} %all-to-all-done.2), kind=kOutput, calls=%fused_computation.35 | convolution fusion | flops 1821560832 | bytes 9609216 | tf_op jit(solution)/shard_map/cop,io->cip/dot_general | solution.py:118
  159.4 10.8 %all-reduce.5 = f32[8,2,200]{2,1,0:T(2,128)S(1)} all-reduce(f32[8,2,200]{2,1,0:T(2,128)S(1)} %fusion.49), channel_id=3, replica_groups=mesh['pix'=4,'exp'=8] {'pix'}, use_global_device_ids=true, to_apply=%region_14.16.clone | all-reduce | flops 3200 | bytes 25600
  176.6 23.5 %custom-call.21 = f32[2,128,128]{2,1,0:T(8,128)S(1)} custom-call(f32[2,128,128]{2,1,0:T(8,128)S(1)} %cholesky.215), custom_call_target="Cholesky" | custom-call | tf_op jit(solution)/shard_map/jit(cholesky)/cholesky | solution.py:15
  201.0 23.5 %custom-call.26 = f32[2,128,128]{2,1,0:T(8,128)S(1)} custom-call(f32[2,128,128]{2,1,0:T(8,128)S(1)} %cholesky.218), custom_call_target="Cholesky" | custom-call | tf_op jit(solution)/shard_map/jit(cholesky)/cholesky | solution.py:15
  225.8 20.3 %custom-call.27 = f32[2,1,128,128]{2,3,1,0:T(8,128)} custom-call(f32[2,1,128,128]{3,2,1,0:T(8,128)S(1)} %get-tuple-element.204), custom_call_target="InvertDiagBlocksLowerTriangular" | custom-call | tf_op jit(solution)/shard_map/jit(cholesky)/cholesky | solution.py:15
  248.5 14.2 %custom-call.28 = f32[2,72,72]{2,1,0:T(8,128)} custom-call(f32[2,72,72]{2,1,0:T(8,128)S(1)} %convolution_subtract_fusion), custom_call_target="Cholesky" | custom-call | tf_op jit(solution)/shard_map/jit(cholesky)/cholesky | solution.py:15
  262.7 20.3 %custom-call.22 = f32[2,1,128,128]{2,3,1,0:T(8,128)} custom-call(f32[2,1,128,128]{3,2,1,0:T(8,128)S(1)} %get-tuple-element.203), custom_call_target="InvertDiagBlocksLowerTriangular" | custom-call | tf_op jit(solution)/shard_map/jit(cholesky)/cholesky | solution.py:15
  286.1 14.0 %custom-call.23 = f32[2,72,72]{2,1,0:T(8,128)S(1)} custom-call(f32[2,72,72]{2,1,0:T(8,128)} %convolution_subtract_fusion.1), custom_call_target="Cholesky" | custom-call | tf_op jit(solution)/shard_map/jit(cholesky)/cholesky | solution.py:15
  304.9 40.1 %custom-call.24 = f32[2,2,128,128]{2,3,1,0:T(8,128)S(1)} custom-call(f32[2,2,128,128]{3,2,1,0:T(8,128)} %pad_maximum_fusion.1), custom_call_target="InvertDiagBlocksLowerTriangular" | custom-call | tf_op jit(solution)/shard_map/jit(_solve_triangular)/vmap()/triangular_solve | solution.py:17
  347.3 39.3 %custom-call.25 = f32[2,2,128,128]{2,3,1,0:T(8,128)S(1)} custom-call(f32[2,2,128,128]{3,2,1,0:T(8,128)S(1)} %copy.119), custom_call_target="InvertDiagBlocksLowerTriangular" | custom-call | tf_op jit(solution)/shard_map/jit(_solve_triangular)/vmap()/triangular_solve | solution.py:18
  389.0 5.2 all_gather.6
  394.7 14.5 %fusion.63 = f32[3,32,384]{2,1,0:T(8,128)S(1)} fusion(f32[3,6144]{1,0:T(4,128)S(1)} %pad_maximum_fusion.7, f32[6144,384]{1,0:T(8,128)} %copy.123, s32[6144]{0:T(1024)S(1)} %bitcast.243), kind=kOutput, calls=%fused_computation.74 | convolution fusion | flops 2725183488 | bytes 9682944 | tf_op jit(solution)/shard_map/cip,io->cop/dot_general | solution.py:54
  412.6 8.5 %all-to-all-done.3 = f32[3,32,384]{2,0,1:T(4,128)S(1)} async-done(((f32[3,32,384]{2,0,1:T(4,128)}), f32[3,32,384]{2,0,1:T(4,128)S(1)}, u32[]{:S(2)}, u32[]{:S(2)}) %all-to-all-start.3) | async-done | bytes 147488 | tf_op jit(solution)/shard_map/all_to_all | solution.py:87
  421.6 13.3 %while.48 = (s32[]{:T(128)}, f32[8,3,768]{2,1,0:T(4,128)S(1)}, f32[8,3,1536]{2,1,0:T(4,128)S(1)}, s32[8,1536]{1,0:T(8,128)S(1)}, s32[]{:T(128)}) while((s32[]{:T(128)}, f32[8,3,768]{2,1,0:T(4,128)S(1)}, f32[8,3,1536]{2,1,0:T(4,128)S(1)}, s32[8,1536]{1,0:T(8,128)S(1)}, s32[]{:T(128)}) %tuple.132), condition=%wide.region_17.21_spmd, body=%wide.region_16.20_spmd.sunk | while | flops 43646976 | bytes 58433 | solution.py:102
  435.7 22.9 %while.49 = (s32[]{:T(128)}, f32[8,2,1536]{2,1,0:T(2,128)}, s32[8,1536]{1,0:T(8,128)S(1)}, f32[2,768]{1,0:T(2,128)S(1)}, s32[]{:T(128)}) while((s32[]{:T(128)}, f32[8,2,1536]{2,1,0:T(2,128)}, s32[8,1536]{1,0:T(8,128)S(1)}, f32[2,768]{1,0:T(2,128)S(1)}, s32[]{:T(128)}) %tuple.133), condition=%wide.region_20.24_spmd, body=%wide.region_19.23_spmd.sunk | while | flops 29491200 | bytes 37441 | solution.py:108
  441.4 2.8 fusion.158
  444.3 2.8 fusion.158
  447.1 2.8 fusion.158
  450.0 2.8 fusion.158
  452.8 2.8 fusion.158
  455.7 2.8 fusion.158
  458.5 3.3 all-to-all-start.4
  461.9 39.9 %custom-call.29 = f32[2,2,128,128]{2,3,1,0:T(8,128)} custom-call(f32[2,2,128,128]{3,2,1,0:T(8,128)S(1)} %pad_maximum_fusion.3), custom_call_target="InvertDiagBlocksLowerTriangular" | custom-call | tf_op jit(solution)/shard_map/jit(_solve_triangular)/vmap()/triangular_solve | solution.py:17
  501.8 39.9 %custom-call.30 = f32[2,2,128,128]{2,3,1,0:T(8,128)} custom-call(f32[2,2,128,128]{3,2,1,0:T(8,128)S(1)} %copy.138), custom_call_target="InvertDiagBlocksLowerTriangular" | custom-call | tf_op jit(solution)/shard_map/jit(_solve_triangular)/vmap()/triangular_solve | solution.py:18
  541.8 10.6 %multiply_reduce_fusion = f32[6144,2]{0,1:T(2,128)S(1)} fusion(f32[6144,384]{0,1:T(8,128)} %fusion.32, s32[6144]{0:T(1024)S(1)} %bitcast.244, f32[2,32,384]{2,0,1:T(2,128)} %all-to-all-done.4), kind=kOutput, calls=%fused_computation.34 | convolution fusion | flops 1821560832 | bytes 9609216 | tf_op jit(solution)/shard_map/cop,io->cip/dot_general | solution.py:118
  553.2 11.3 %all-reduce.6 = f32[8,2,200]{2,1,0:T(2,128)S(1)} all-reduce(f32[8,2,200]{2,1,0:T(2,128)S(1)} %fusion.38), channel_id=5, replica_groups=mesh['pix'=4,'exp'=8] {'pix'}, use_global_device_ids=true, to_apply=%region_22.26.clone | all-reduce | flops 3200 | bytes 25600
  568.4 5.2 all_gather.7
  (210 shorter events, 84.4 us)
Async XLA Ops:
  7.2 163.6 %reduce-scatter.3.cloned.1.call-start = ((), (), s32[]{:S(2)}) async-start(), calls=%async_computation.7 | async-start | bytes 2048000 | tf_op jit(solution)/shard_map/reduce_scatter | solution.py:127
  8.9 4.0 copy-start.10
  8.9 5.5 copy-start
  12.9 1.5 copy-start.2
  14.4 2.2 copy-start.8
  17.5 18.1 %copy-start.18 = (s32[6144]{0:T(1024)S(1)}, s32[6144]{0:T(1024)}, u32[]{:S(2)}) copy-start(s32[6144]{0:T(1024)} %param.25) | copy-start | bytes 73732
  41.9 43.7 %all-to-all-start = ((s32[32,1,384]{2,1,0:T(1,128)}), s32[32,1,384]{2,1,0:T(1,128)S(1)}, u32[]{:S(2)}, u32[]{:S(2)}) async-start(s32[32,1,384]{2,1,0:T(1,128)} %copy.121), calls=%async_computation.1 | async-start | bytes 98304 | tf_op jit(solution)/shard_map/all_to_all | solution.py:58
  49.1 121.6 %reduce-scatter.5.cloned.1.call-start = ((), (), s32[]{:S(2)}) async-start(), calls=%async_computation.8 | async-start | bytes 2048000 | tf_op jit(solution)/shard_map/reduce_scatter | solution.py:127
  58.2 9.7 %copy-start.23 = (f32[8,2,200]{2,1,0:T(2,128)S(1)}, f32[8,2,200]{2,1,0:T(2,128)}, u32[]{:S(2)}) copy-start(f32[8,2,200]{2,1,0:T(2,128)} %param.26) | copy-start | bytes 38404
  68.5 15.3 %copy-start.24 = (u32[32]{0:T(128)S(1)}, u32[32]{0:T(128)}, u32[]{:S(2)}) copy-start(u32[32]{0:T(128)} %constant.218) | copy-start | bytes 388
  85.6 14.4 %all-to-all-start.1 = ((f32[3,32,384]{2,0,1:T(4,128)}), f32[3,32,384]{2,0,1:T(4,128)S(1)}, u32[]{:S(2)}, u32[]{:S(2)}) async-start(f32[3,32,384]{2,0,1:T(4,128)} %copy.124), calls=%async_computation.2 | async-start | bytes 393216 | tf_op jit(solution)/shard_map/all_to_all | solution.py:87
  100.3 13.4 %copy-start.16 = (f32[768]{0:T(1024)S(1)}, f32[768]{0:T(1024)}, u32[]{:S(2)}) copy-start(f32[768]{0:T(1024)} %param.28) | copy-start | bytes 9220
  100.4 13.4 %copy-start.19 = (f32[2,768]{1,0:T(2,128)S(1)}, f32[2,768]{1,0:T(2,128)}, u32[]{:S(2)}) copy-start(f32[2,768]{1,0:T(2,128)} %param.27) | copy-start | bytes 18436
  137.4 10.6 %all-to-all-start.2 = ((f32[2,32,384]{2,0,1:T(2,128)}), f32[2,32,384]{2,0,1:T(2,128)S(1)}, u32[]{:S(2)}, u32[]{:S(2)}) async-start(f32[2,32,384]{2,0,1:T(2,128)} %bitcast.32), calls=%async_computation.3 | async-start | bytes 196608 | tf_op jit(solution)/shard_map/all_to_all | solution.py:109
  148.0 10.6 %copy-start.3 = (bf16[200,6144]{1,0:T(8,128)(2,1)S(1)}, bf16[200,6144]{1,0:T(8,128)(2,1)}, u32[]{:S(2)}) copy-start(bf16[200,6144]{1,0:T(8,128)(2,1)} %copy-done.2) | copy-start | bytes 7372804
  172.0 52.5 %copy-start.15 = (pred[128,128]{1,0:T(8,128)(4,1)S(1)}, pred[128,128]{1,0:T(8,128)(4,1)}, u32[]{:S(2)}) copy-start(pred[128,128]{1,0:T(8,128)(4,1)} %get-tuple-element.219) | copy-start | bytes 49156
  175.9 0.8 copy-start.7
  175.9 125.6 %copy-start.12 = (pred[200,200]{1,0:T(8,128)(4,1)S(1)}, pred[200,200]{1,0:T(8,128)(4,1)}, u32[]{:S(2)}) copy-start(pred[200,200]{1,0:T(8,128)(4,1)} %iota_compare_fusion.29) | copy-start | bytes 120004
  225.8 75.3 %copy-start.22 = (f32[2,128]{1,0:T(2,128)S(1)}, f32[2,128]{1,0:T(2,128)}, u32[]{:S(2)}) copy-start(f32[2,128]{1,0:T(2,128)} %get-tuple-element.150) | copy-start | bytes 3076
  301.7 0.8 copy-start.4
  301.7 0.9 copy-start.6
  304.2 90.5 %copy-start.11 = (f32[6144]{0:T(1024)S(1)}, f32[6144]{0:T(1024)}, u32[]{:S(2)}) copy-start(f32[6144]{0:T(1024)} %copy-done.10) | copy-start | bytes 73732
  394.1 15.1 %copy-start.14 = (f32[8,2,200]{2,1,0:T(2,128)}, f32[8,2,200]{2,1,0:T(2,128)S(1)}, u32[]{:S(2)}) copy-start(f32[8,2,200]{2,1,0:T(2,128)S(1)} %all_gather.6) | copy-start | bytes 38404
  394.7 17.9 %copy-start.5 = (f32[2,200,200]{2,1,0:T(8,128)S(1)}, f32[2,200,200]{2,1,0:T(8,128)}, u32[]{:S(2)}) copy-start(f32[2,200,200]{2,1,0:T(8,128)} %copy-done.4) | copy-start | bytes 960004
  410.0 11.1 %all-to-all-start.3 = ((f32[3,32,384]{2,0,1:T(4,128)}), f32[3,32,384]{2,0,1:T(4,128)S(1)}, u32[]{:S(2)}, u32[]{:S(2)}) async-start(f32[3,32,384]{2,0,1:T(4,128)} %copy.141), calls=%async_computation.5 | async-start | bytes 393216 | tf_op jit(solution)/shard_map/all_to_all | solution.py:87
  421.5 13.4 %copy-start.17 = (f32[768]{0:T(1024)S(1)}, f32[768]{0:T(1024)}, u32[]{:S(2)}) copy-start(f32[768]{0:T(1024)} %param.28) | copy-start | bytes 9220
  421.5 13.4 %copy-start.20 = (f32[2,768]{1,0:T(2,128)S(1)}, f32[2,768]{1,0:T(2,128)}, u32[]{:S(2)}) copy-start(f32[2,768]{1,0:T(2,128)} %param.27) | copy-start | bytes 18436
  435.7 26.2 %copy-start.9 = (f32[2,1,128,128]{3,2,1,0:T(8,128)S(1)}, f32[2,1,128,128]{3,2,1,0:T(8,128)}, u32[]{:S(2)}) copy-start(f32[2,1,128,128]{3,2,1,0:T(8,128)} %get-tuple-element.192) | copy-start | bytes 393220
  458.5 3.3 copy-start.21
  458.5 83.3 %all-to-all-start.4 = ((f32[2,32,384]{2,0,1:T(2,128)}), f32[2,32,384]{2,0,1:T(2,128)}, u32[]{:S(2)}, u32[]{:S(2)}) async-start(f32[2,32,384]{2,0,1:T(2,128)} %bitcast.58), calls=%async_computation.6 | async-start | bytes 196608 | tf_op jit(solution)/shard_map/all_to_all | solution.py:109
  541.8 10.6 %copy-start.1 = (bf16[200,6144]{1,0:T(8,128)(2,1)S(1)}, bf16[200,6144]{1,0:T(8,128)(2,1)}, u32[]{:S(2)}) copy-start(bf16[200,6144]{1,0:T(8,128)(2,1)} %get-tuple-element.186) | copy-start | bytes 7372804
  552.4 12.1 %copy-start.13 = (f32[2,2,128,128]{2,3,1,0:T(8,128)S(1)}, f32[2,2,128,128]{2,3,1,0:T(8,128)}, u32[]{:S(2)}) copy-start(f32[2,2,128,128]{2,3,1,0:T(8,128)} %custom-call.29) | copy-start | bytes 786436
Sparse Core Ops, SparseCore 0:
  16.7 31.3 reduce-scatter.2
  53.6 29.8 reduce-scatter.4
where the time goes:
time: 590 us; the launch traced here: 581 us
  other arithmetic  316 us (54%)
  matrix products  148 us (25%)
  blocking collectives  32.5 us (6%)
  local copies, waits for them, and re-layouts  23.9 us (4%)
  waiting for transfers between devices  22.6 us (4%)
  starting transfers between devices  22.5 us (4%)
  between operations  15.5 us (3%)
    another operation x16, other arithmetic, solve_blocks(): factor = jnp.linalg.cholesky(gram_block + RIDGE * identity)  120 us
    another operation x9, other arithmetic, solve_blocks(): jax.scipy.linalg.solve_triangular(factor, middle, lower=True, trans=1)  81.5 us
    another operation x4, other arithmetic, solve_blocks(): middle = jax.scipy.linalg.solve_triangular(factor, columns, lower=True)  80.8 us
    dot_general x16, matrix products, lookup(): jnp.dot(star_means, star_table(id_block, star_count).T, precision=highest)  45.3 us
    dot_general x3, matrix products, place(): placed = jnp.einsum('cip,io->cop', spread, owner_hot, precision=highest)  34.5 us
    dot_general x16, matrix products, accumulate(): jnp.dot(value_block, star_table(id_block, star_count), precision=highest)  26.1 us
    unnamed x2, blocking collectives  22.1 us
    dot_general x2, matrix products, on_device(): jnp.einsum('cop,io->cip', shaped, owner_hot, precision=highest)  21.2 us
  transfers between devices with their start and end apart: 7, of which 3 were waited for; matrix products, arithmetic and copies ran while one was open for 33% of the time, Pallas kernels for 0%

commit v1 on v0

v1 whole, which is shorter than its diff:
```python
import functools

import jax
import jax.numpy as jnp
from jax import lax
from jax.experimental import pallas as pl
from jax.experimental.pallas import tpu as pltpu
from jax.sharding import PartitionSpec as P

ITERS = 2
RIDGE = 0.5
LANES = 128
PIVOTS = 40
VMEM_BYTES = 50 * 1024 * 1024


def split_two(x):
    high = x.astype(jnp.bfloat16)
    low = (x - high.astype(jnp.float32)).astype(jnp.bfloat16)
    return high, low


def slot_table(slot_row, star_count):
    ids = lax.broadcasted_iota(jnp.int32, (star_count, slot_row.shape[1]), 0)
    return jnp.where(ids == slot_row, 1.0, 0.0).astype(jnp.bfloat16)


def dot_last(a, b):
    return lax.dot_general(a, b, (((1,), (1,)), ((), ())), preferred_element_type=jnp.float32)


def scatter_block(values, owner_row, slot_row, peers, star_count):
    hot = lax.broadcasted_iota(jnp.int32, (peers, owner_row.shape[1]), 0) == owner_row
    parts = []
    for value in values:
        high = value.astype(jnp.bfloat16).astype(jnp.float32)
        for part in (high, value - high):
            parts.append(jnp.where(hot, part, 0.0).astype(jnp.bfloat16))
    table = slot_table(slot_row, star_count)
    return dot_last(jnp.concatenate(parts, axis=0), table)


def sums_kernel(
    peers, chosen, design_ref, weight_ref, mask_ref, owner_ref, slot_ref, coef_ref, *out_refs
):
    predicted_ref, sums_ref = out_refs[-2:]
    maps_device = coef_ref.shape[0]
    width = design_ref.shape[1] // maps_device
    count, _, star_count = sums_ref.shape

    def block(j, total):
        at = pl.ds(pl.multiple_of(j * width, width), width)
        design = design_ref[:, at]
        weights = [weight_ref[:, at] * mask_ref[k : k + 1, at].astype(jnp.float32) for k in chosen]
        if len(chosen) > 1:
            wide = design.astype(jnp.float32)
            for k in range(len(chosen)):
                weighted = (wide * weights[k]).astype(jnp.bfloat16)
                out_refs[0][k, j] = dot_last(weighted, design)
        maps = coef_ref[j].astype(jnp.bfloat16)
        predicted = jnp.dot(maps, design, preferred_element_type=jnp.float32)
        predicted_ref[:, at] = predicted
        values = [predicted[c : c + 1] * weights[0] for c in range(2)]
        if len(chosen) > 1:
            values = values + weights
        return total + scatter_block(
            values, owner_ref[:, at], slot_ref[:, at], peers, star_count
        )

    total = lax.fori_loop(
        0, maps_device, block, jnp.zeros((2 * count * peers, star_count), jnp.float32)
    )
    for v in range(count):
        at = 2 * v * peers
        sums_ref[v] = total[at : at + peers] + total[at + peers : at + 2 * peers]


def right_kernel(
    peers, design_ref, weight_ref, mask_ref, owner_ref, slot_ref, predicted_ref, means_ref,
    right_ref, split_ref,
):
    @pl.when(pl.program_id(0) == 0)
    def _():
        for c in range(2):
            high, low = split_two(means_ref[c])
            split_ref[2 * c * peers : (2 * c + 1) * peers] = high
            split_ref[(2 * c + 1) * peers : (2 * c + 2) * peers] = low

    owner_row = owner_ref[...]
    table = slot_table(slot_ref[...], split_ref.shape[1])
    found = jnp.dot(split_ref[...], table, preferred_element_type=jnp.float32)
    hot = lax.broadcasted_iota(jnp.int32, (peers, owner_row.shape[1]), 0) == owner_row
    rows = []
    for c in range(2):
        at = 2 * c * peers
        both = found[at : at + peers] + found[at + peers : at + 2 * peers]
        mean = jnp.sum(jnp.where(hot, both, 0.0), axis=0, keepdims=True)
        rows.append(mean - predicted_ref[c : c + 1, :])
    residual = jnp.concatenate(rows, axis=0).astype(jnp.bfloat16)
    weight = weight_ref[...] * mask_ref[...].astype(jnp.float32)
    weighted = (design_ref[...].astype(jnp.float32) * weight).astype(jnp.bfloat16)
    right_ref[0] = dot_last(residual, weighted)


def sweep_panel(panels):
    lane = lax.broadcasted_iota(jnp.int32, (8, LANES), 1)
    row = lax.broadcasted_iota(jnp.int32, (8, LANES), 0)
    for s in range(PIVOTS):
        tile, sub = s // 8, s % 8
        swept = []
        for panel in panels:
            columns = [jnp.broadcast_to(t[0][:, s : s + 1], (8, LANES)) for t in panel]
            pivot = jnp.broadcast_to(columns[tile][sub : sub + 1, :], (8, LANES))
            inverse = 1.0 / pivot
            fresh = [
                jnp.broadcast_to(half[sub : sub + 1, :], (8, LANES)) * inverse
                for half in panel[tile]
            ]
            fresh[0] = jnp.where(lane == s, -inverse, fresh[0])
            done = []
            for t in range(len(panel)):
                halves = []
                for h in range(len(panel[t])):
                    old = jnp.where(lane == s, 0.0, panel[t][h]) if h == 0 else panel[t][h]
                    new = old - columns[t] * fresh[h]
                    if t == tile:
                        new = jnp.where(row == sub, fresh[h], new)
                    halves.append(new)
                done.append(halves)
            swept.append(done)
        panels = swept
    return panels


def inverse_kernel(gram_ref, out_ref, work_ref):
    count, size = gram_ref.shape[0], gram_ref.shape[1]
    span = work_ref.shape[2]
    tiles = PIVOTS // 8
    halves = span // LANES
    diagonal = lax.broadcasted_iota(jnp.int32, (size, size), 0) == lax.broadcasted_iota(
        jnp.int32, (size, size), 1
    )
    work_ref[...] = jnp.zeros_like(work_ref)
    for m in range(count):
        gram = gram_ref[m]
        work_ref[m, :size, :size] = 0.5 * (gram + gram.T) + jnp.where(diagonal, RIDGE, 0.0)

    def block(_, carry):
        panels = [
            [
                [work_ref[m, 8 * t : 8 * t + 8, LANES * h : LANES * (h + 1)] for h in range(halves)]
                for t in range(tiles)
            ]
            for m in range(count)
        ]
        swept = sweep_panel(panels)
        for m in range(count):
            before = work_ref[m, :PIVOTS, :]
            after = jnp.concatenate(
                [jnp.concatenate(tile, axis=1) for tile in swept[m]], axis=0
            )
            change = lax.dot_general(
                before, after, (((0,), (0,)), ((), ())),
                precision=lax.Precision.HIGHEST, preferred_element_type=jnp.float32,
            )
            lanes = lax.broadcasted_iota(jnp.int32, (span - PIVOTS, span), 1)
            rest = jnp.where(lanes < PIVOTS, 0.0, work_ref[m, PIVOTS:, :]) - change[PIVOTS:, :]
            work_ref[m, : span - PIVOTS, :] = pltpu.roll(rest, span - PIVOTS, 1)
            work_ref[m, span - PIVOTS :, :] = pltpu.roll(after, span - PIVOTS, 1)
        return carry

    lax.fori_loop(0, size // PIVOTS, block, 0)
    start = span - size
    for m in range(count):
        turned = pltpu.roll(work_ref[m, start:, :], size, 1)
        out_ref[m] = -turned[:, :size]


def invert(grams):
    count, size = grams.shape[0], grams.shape[1]
    span = -(-size // LANES) * LANES
    return pl.pallas_call(
        inverse_kernel,
        out_shape=jax.ShapeDtypeStruct((count, size, size), jnp.float32),
        in_specs=[pl.BlockSpec(memory_space=pltpu.VMEM)],
        out_specs=pl.BlockSpec(memory_space=pltpu.VMEM),
        scratch_shapes=[pltpu.VMEM((count, span, span), jnp.float32)],
        compiler_params=pltpu.CompilerParams(vmem_limit_bytes=VMEM_BYTES),
    )(grams)


def on_device(
    design, det_weight, outlier_mask, star_owner, star_slot, coef_init, star_ref, star_prior
):
    highest = lax.Precision.HIGHEST
    peers = lax.axis_size(("pix", "exp"))
    pix_count = lax.axis_size("pix")
    terms, rows = design.shape
    maps_device = coef_init.shape[0]
    width = rows // maps_device
    star_count = star_prior.shape[0]
    share = maps_device // pix_count
    weight_row = det_weight.reshape(1, rows)
    owner_row = star_owner.reshape(1, rows)
    slot_row = star_slot.reshape(1, rows)
    params = pltpu.CompilerParams(vmem_limit_bytes=VMEM_BYTES)

    def line(count):
        return pl.BlockSpec((count, width), lambda j: (0, j))

    maps_spec = pl.BlockSpec((1, 2, terms), lambda j: (j, 0, 0))

    def whole(shape):
        return pl.BlockSpec(shape, lambda j: (0,) * len(shape))

    f32 = jnp.float32
    def sums_call(chosen, coefficients):
        count = 2 + (len(chosen) if len(chosen) > 1 else 0)
        shapes = [
            jax.ShapeDtypeStruct((2, rows), f32),
            jax.ShapeDtypeStruct((count, peers, star_count), f32),
        ]
        if len(chosen) > 1:
            shapes.insert(0, jax.ShapeDtypeStruct((ITERS, maps_device, terms, terms), f32))
        vmem = pl.BlockSpec(memory_space=pltpu.VMEM)
        return pl.pallas_call(
            functools.partial(sums_kernel, peers, chosen),
            out_shape=tuple(shapes),
            in_specs=[vmem] * 6,
            out_specs=(vmem,) * len(shapes),
            compiler_params=params,
        )(design, weight_row, outlier_mask, owner_row, slot_row, coefficients)

    grams, predicted, sums = sums_call(tuple(range(ITERS)), coef_init)
    own_grams = lax.psum_scatter(grams, "pix", scatter_dimension=1, tiled=True)
    inverses = invert(own_grams.reshape(ITERS * share, terms, terms)).reshape(own_grams.shape)
    coefficients = coef_init
    bottoms = None
    for k in range(ITERS):
        mask_row = outlier_mask[k : k + 1]
        if k > 0:
            predicted, sums = sums_call((k,), coefficients)
        arrived = lax.all_to_all(
            sums, ("pix", "exp"), split_axis=1, concat_axis=1, tiled=True
        )
        totals = jnp.sum(arrived, axis=1)
        if k == 0:
            bottoms = totals[2:]
        star_means = (star_prior * star_ref + totals[:2]) / (star_prior + bottoms[k])
        all_means = lax.all_gather(star_means, ("pix", "exp"), axis=1, tiled=False)
        right = pl.pallas_call(
            functools.partial(right_kernel, peers),
            grid=(maps_device,),
            out_shape=jax.ShapeDtypeStruct((maps_device, 2, terms), f32),
            in_specs=[
                line(terms), line(1), line(1), line(1), line(1), line(2),
                whole((2, peers, star_count)),
            ],
            out_specs=maps_spec,
            scratch_shapes=[pltpu.VMEM((4 * peers, star_count), jnp.bfloat16)],
            compiler_params=params,
        )(design, weight_row, mask_row, owner_row, slot_row, predicted, all_means)
        own_right = lax.psum_scatter(right, "pix", scatter_dimension=0, tiled=True)
        own_maps = lax.dynamic_slice_in_dim(
            coefficients, lax.axis_index("pix") * share, share, 0
        )
        update = jnp.einsum("ect,etu->ecu", own_right, inverses[k], precision=highest)
        coefficients = lax.all_gather(own_maps + update, "pix", axis=0, tiled=True)
    return (coefficients, star_means)


def solution(mesh):
    placed = (
        P(None, ("pix", "exp")),
        P(("pix", "exp")),
        P(None, ("pix", "exp")),
        P(("pix", "exp"), None),
        P(("pix", "exp")),
        P("exp", None, None),
        P(None, ("pix", "exp")),
        P(("pix", "exp")),
    )
    return jax.shard_map(
        on_device,
        mesh=mesh,
        in_specs=placed,
        out_specs=(P("exp", None, None), P(None, ("pix", "exp"))),
        check_vma=False,
    )
```

time: 590 us -> 280 us (0.47); the launches traced: 581 us -> 279 us
  other arithmetic: 316 us -> 2.11 us
  matrix products: 148 us -> 1.32 us
  blocking collectives: 32.5 us -> 175 us
  Pallas kernels: 0 us -> 57.2 us
  starting transfers between devices: 22.5 us -> 7.41 us
  local copies, waits for them, and re-layouts: 23.9 us -> 9.11 us
  waiting for transfers between devices: 22.6 us -> 12.2 us
    another operation x32 -> x0, other arithmetic: 299 us -> none  [the longest x16 120 us: solve_blocks(): factor = jnp.linalg.cholesky(gram_block + RIDGE * identity)]
    dot_general x43 -> x2, matrix products: 135 us -> 1.32 us  [on_device(): jnp.einsum('ect,etu->ecu', own_right, inverses[k], precision=highest)]
    all_gather x2 -> x4, blocking collectives: 10.3 us -> 144 us  [the longest x2 133 us: on_device(): all_means = lax.all_gather(star_means, ('pix', 'exp'), axis=1, tiled=False)]
    pallas_call x0 -> x5, Pallas kernels: none -> 57.2 us  [the longest x1 35.2 us: invert(): pl.pallas_call(inverse_kernel, out_shape=jax.ShapeDtypeStruct((count, siz...]
    all_to_all x5 -> x1, starting transfers between devices: 22 us -> 7.37 us  [on_device(): lax.all_to_all(sums, ('pix', 'exp'), split_axis=1, concat_axis=1, tiled=T...]
    another operation x16 -> x0, matrix products: 12.4 us -> none  [the longest x4 5.38 us: solve_blocks(): factor = jnp.linalg.cholesky(gram_block + RIDGE * identity)]
    all_to_all x5 -> x1, waiting for transfers between devices: 22.6 us -> 11.5 us  [on_device(): lax.all_to_all(sums, ('pix', 'exp'), split_axis=1, concat_axis=1, tiled=T...]
    all_to_all x0 -> x1, blocking collectives: none -> 10.9 us  [on_device(): lax.all_to_all(sums, ('pix', 'exp'), split_axis=1, concat_axis=1, tiled=T...]
  transfers between devices with their start and end apart: 7 -> 2, of which waited for: 3 -> 1; matrix products, arithmetic and copies ran while one was open for 33% -> 1% of each run, Pallas kernels for 0% -> 2%
where the time goes in v1:
time: 280 us; the launch traced here: 279 us
  blocking collectives  175 us (62%)
  Pallas kernels  57.2 us (20%)
  between operations  14.9 us (5%)
  waiting for transfers between devices  12.2 us (4%)
  local copies, waits for them, and re-layouts  9.11 us (3%)
  starting transfers between devices  7.41 us (3%)
    all_gather x2, blocking collectives, on_device(): all_means = lax.all_gather(star_means, ('pix', 'exp'), axis=1, tiled=False)  133 us
    pallas_call x1, Pallas kernels, invert(): pl.pallas_call(inverse_kernel, out_shape=jax.ShapeDtypeStruct((count, siz...  35.2 us
    unnamed x2, blocking collectives  20.2 us
    pallas_call x2, Pallas kernels, sums_call(): pl.pallas_call(functools.partial(sums_kernel, peers, chosen), out_shape=t...  13.5 us
    all_to_all x1, waiting for transfers between devices, on_device(): lax.all_to_all(sums, ('pix', 'exp'), split_axis=1, concat_axis=1, tiled=T...  11.5 us
    all_to_all x1, blocking collectives, on_device(): lax.all_to_all(sums, ('pix', 'exp'), split_axis=1, concat_axis=1, tiled=T...  10.9 us
    all_gather x2, blocking collectives, on_device(): coefficients = lax.all_gather(own_maps + update, 'pix', axis=0, tiled=True)  10.3 us
    pallas_call x2, Pallas kernels, on_device(): pl.pallas_call(functools.partial(right_kernel, peers), grid=(maps_device,...  8.51 us
  transfers between devices with their start and end apart: 2, of which 1 were waited for; matrix products, arithmetic and copies ran while one was open for 1% of the time, Pallas kernels for 2%

profile of v1, /device:TPU:0, one launch (start us, length us, event | category | flops | bytes accessed | tf_op | source)
XLA Modules:
  0.0 278.9 jit_solution(5397818283208321669)
XLA Ops:
  7.2 0.0 copy-start
  7.2 1.7 copy-done
  8.9 0.0 copy-start.2
  8.9 0.8 copy-done.2
  9.7 0.0 copy-start.4
  9.7 0.7 copy-done.4
  10.4 0.0 copy-start.6
  10.4 0.7 copy-done.6
  11.1 0.0 copy-start.8
  11.1 0.7 copy-done.8
  11.9 0.7 copy-done.10
  12.6 8.4 %shard_map.95 = (f32[2,8,200,200]{3,2,1,0:T(8,128)}, f32[2,6144]{1,0:T(2,128)S(1)}, f32[4,32,768]{2,1,0:T(8,128)S(1)}) custom-call(bf16[200,6144]{1,0:T(8,128)(2,1)S(1)} %copy-done, f32[1,6144]{1,0:T(1,128)S(1)} %bitcast.18, s32[2,6144]{1,0:T(2,128)S(1)} %copy-done.2, s32[1,6144]{1,0:T(1,128)S(1)} %bitcast.22, s32[1,6144]{1,0:T(1,128)S(1)} %bitcast.26, ...), custom_call_target="tpu_custom_call" | custom-call | tf_op jit(solution)/shard_map/pallas_call | solution.py:226
  21.0 0.0 copy-start.7
  21.0 0.0 copy-start.9
  21.1 1.0 copy.10
  22.1 7.4 %all-to-all-start = ((f32[4,32,768]{2,0,1:T(4,128)}), f32[4,32,768]{2,0,1:T(4,128)}, u32[]{:S(2)}, u32[]{:S(2)}) async-start(f32[4,32,768]{2,0,1:T(4,128)} %copy.10), calls=%async_computation | async-start | bytes 786432 | tf_op jit(solution)/shard_map/all_to_all | solution.py:243
  29.5 0.0 all-reduce.5.cloned.1.call-start
  29.5 0.7 all-reduce.5.cloned.1.call-update
  30.2 0.0 copy-done.3
  30.3 0.0 copy-done.14
  30.3 0.6 dynamic-slice
  31.5 11.5 %all-to-all-done = f32[4,32,768]{2,0,1:T(4,128)} async-done(((f32[4,32,768]{2,0,1:T(4,128)}), f32[4,32,768]{2,0,1:T(4,128)}, u32[]{:S(2)}, u32[]{:S(2)}) %all-to-all-start) | async-done | bytes 393248 | tf_op jit(solution)/shard_map/all_to_all | solution.py:243
  43.0 1.1 reduce_sum.18
  44.1 0.0 copy-done.11
  44.1 0.0 copy-done.13
  44.2 66.7 %all-gather = f32[2,24576]{1,0:T(2,128)S(1)} all-gather(f32[2,768]{1,0:T(2,128)S(1)} %fusion.2), channel_id=2, replica_groups=mesh['pix'=4,'exp'=8] {'pix','exp'}, dimensions={1}, use_global_device_ids=true | all-gather | bytes 202752 | tf_op jit(solution)/shard_map/all_gather | solution.py:250
  110.9 0.0 copy-done.1
  110.9 0.0 copy-done.5
  110.9 0.0 copy-done.7
  110.9 0.0 copy-done.9
  110.9 4.3 %shard_map.96 = f32[8,2,200]{2,1,0:T(2,128)S(1)} custom-call(bf16[200,6144]{1,0:T(8,128)(2,1)S(1)} %copy-done.1, f32[1,6144]{1,0:T(1,128)S(1)} %bitcast.19, s32[1,6144]{1,0:T(1,128)S(1)} %get-tuple-element.14.mask_ref, s32[1,6144]{1,0:T(1,128)S(1)} %bitcast.23, s32[1,6144]{1,0:T(1,128)S(1)} %bitcast.27, f32[2,6144]{1,0:T(2,128)S(1)} %get-tuple-element.7.predicted_ref, ...), custom_call_target="tpu_custom_call" | custom-call | tf_op jit(solution)/shard_map/pallas_call | solution.py:251
  115.2 10.1 %all-reduce = f32[8,2,200]{2,1,0:T(2,128)S(1)} all-reduce(f32[8,2,200]{2,1,0:T(2,128)S(1)} %shard_map.96), channel_id=4, replica_groups=mesh['pix'=4,'exp'=8] {'pix'}, use_global_device_ids=true, to_apply=%region_1.0.clone | all-reduce | flops 3200 | bytes 25600
  125.3 1.2 constant_dynamic-slice_fusion
  126.5 35.2 %shard_map.97 = f32[4,200,200]{2,1,0:T(8,128)S(1)} custom-call(f32[4,200,200]{2,1,0:T(8,128)S(1)} %bitcast.15), custom_call_target="tpu_custom_call" | custom-call | tf_op jit(solution)/shard_map/pallas_call | solution.py:182
  161.7 1.0 convolution_add_fusion.1
  162.7 5.2 %all_gather.20.coef_ref = f32[8,2,200]{2,1,0:T(2,128)S(1)} all-gather(f32[2,2,200]{2,1,0:T(2,128)S(1)} %convolution_add_fusion.1), channel_id=1, replica_groups=mesh['pix'=4,'exp'=8] {'pix'}, dimensions={0}, use_global_device_ids=true | all-gather | bytes 16000 | tf_op jit(solution)/shard_map/all_gather | solution.py:268
  167.9 5.1 %shard_map.98 = (f32[2,6144]{1,0:T(2,128)S(1)}, f32[2,32,768]{2,1,0:T(8,128)S(1)}) custom-call(bf16[200,6144]{1,0:T(8,128)(2,1)S(1)} %copy-done.1, f32[1,6144]{1,0:T(1,128)S(1)} %bitcast.20, s32[2,6144]{1,0:T(2,128)S(1)} %copy-done.3, s32[1,6144]{1,0:T(1,128)S(1)} %bitcast.24, s32[1,6144]{1,0:T(1,128)S(1)} %bitcast.28, f32[8,2,200]{2,1,0:T(2,128)S(1)} %all_gather.20.coef_ref), custom_call_target="tpu_custom_call" | custom-call | tf_op jit(solution)/shard_map/pallas_call | solution.py:226
  173.0 0.2 copy.11
  173.2 10.9 %all_to_all.10 = f32[2,32,768]{2,0,1:T(2,128)} all-to-all(f32[2,32,768]{2,0,1:T(2,128)S(1)} %copy.11), channel_id=1, replica_groups=mesh['pix'=4,'exp'=8] {'pix','exp'}, dimensions={1} | all-to-all | bytes 393216 | tf_op jit(solution)/shard_map/all_to_all | solution.py:243
  184.1 1.0 reduce_sum.19
  185.1 0.0 copy-start.12
  185.1 66.4 %all-gather.1 = f32[2,24576]{1,0:T(2,128)S(1)} all-gather(f32[2,768]{1,0:T(2,128)S(1)} %add_divide_fusion), channel_id=3, replica_groups=mesh['pix'=4,'exp'=8] {'pix','exp'}, dimensions={1}, use_global_device_ids=true | all-gather | bytes 202752 | tf_op jit(solution)/shard_map/all_gather | solution.py:250
  251.6 4.3 %shard_map.99 = f32[8,2,200]{2,1,0:T(2,128)S(1)} custom-call(bf16[200,6144]{1,0:T(8,128)(2,1)S(1)} %copy-done.1, f32[1,6144]{1,0:T(1,128)S(1)} %bitcast.21, s32[1,6144]{1,0:T(1,128)S(1)} %get-tuple-element.15.mask_ref, s32[1,6144]{1,0:T(1,128)S(1)} %bitcast.25, s32[1,6144]{1,0:T(1,128)S(1)} %bitcast.29, f32[2,6144]{1,0:T(2,128)S(1)} %get-tuple-element.10.predicted_ref, ...), custom_call_target="tpu_custom_call" | custom-call | tf_op jit(solution)/shard_map/pallas_call | solution.py:251
  255.8 10.1 %all-reduce.2 = f32[8,2,200]{2,1,0:T(2,128)S(1)} all-reduce(f32[8,2,200]{2,1,0:T(2,128)S(1)} %shard_map.99), channel_id=6, replica_groups=mesh['pix'=4,'exp'=8] {'pix'}, use_global_device_ids=true, to_apply=%region_4.0.clone | all-reduce | flops 3200 | bytes 25600
  266.0 0.3 convolution_add_fusion
  266.3 5.2 %all_gather.23 = f32[8,2,200]{2,1,0:T(2,128)S(1)} all-gather(f32[2,2,200]{2,1,0:T(2,128)S(1)} %convolution_add_fusion), channel_id=1, replica_groups=mesh['pix'=4,'exp'=8] {'pix'}, dimensions={0}, use_global_device_ids=true | all-gather | bytes 16000 | tf_op jit(solution)/shard_map/all_gather | solution.py:268
  271.5 0.6 copy.22
  272.1 0.0 copy-done.12
  (15 shorter events, 0.1 us)
Async XLA Ops:
  7.2 1.7 copy-start
  8.9 0.8 copy-start.2
  9.7 0.7 copy-start.4
  10.4 0.7 copy-start.6
  11.1 0.7 copy-start.8
  11.9 0.7 copy-start.10
  12.6 17.6 %copy-start.3 = (s32[2,6144]{1,0:T(2,128)S(1)}, s32[2,6144]{1,0:T(2,128)}, u32[]{:S(2)}) copy-start(s32[2,6144]{1,0:T(2,128)} %mask_ref.3) | copy-start | bytes 147460
  12.6 17.7 %copy-start.14 = (u32[32]{0:T(128)S(1)}, u32[32]{0:T(128)}, u32[]{:S(2)}) copy-start(u32[32]{0:T(128)} %constant.15) | copy-start | bytes 388
  21.0 23.1 %copy-start.11 = (f32[768]{0:T(1024)S(1)}, f32[768]{0:T(1024)}, u32[]{:S(2)}) copy-start(f32[768]{0:T(1024)} %param.15) | copy-start | bytes 9220
  21.0 23.1 %copy-start.13 = (f32[2,768]{1,0:T(2,128)S(1)}, f32[2,768]{1,0:T(2,128)}, u32[]{:S(2)}) copy-start(f32[2,768]{1,0:T(2,128)} %param.14) | copy-start | bytes 18436
  21.0 89.9 %copy-start.1 = (bf16[200,6144]{1,0:T(8,128)(2,1)S(1)}, bf16[200,6144]{1,0:T(8,128)(2,1)}, u32[]{:S(2)}) copy-start(bf16[200,6144]{1,0:T(8,128)(2,1)} %design_ref.7) | copy-start | bytes 7372804
  21.0 89.9 %copy-start.5 = (f32[6144]{0:T(1024)S(1)}, f32[6144]{0:T(1024)}, u32[]{:S(2)}) copy-start(f32[6144]{0:T(1024)} %param.9) | copy-start | bytes 73732
  21.0 89.9 %copy-start.7 = (s32[6144,1]{0,1:T(1,128)S(1)}, s32[6144,1]{0,1:T(1,128)}, u32[]{:S(2)}) copy-start(s32[6144,1]{0,1:T(1,128)} %param.11) | copy-start | bytes 73732
  21.0 89.9 %copy-start.9 = (s32[6144]{0:T(1024)S(1)}, s32[6144]{0:T(1024)}, u32[]{:S(2)}) copy-start(s32[6144]{0:T(1024)} %param.12) | copy-start | bytes 73732
  22.1 20.9 %all-to-all-start = ((f32[4,32,768]{2,0,1:T(4,128)}), f32[4,32,768]{2,0,1:T(4,128)}, u32[]{:S(2)}, u32[]{:S(2)}) async-start(f32[4,32,768]{2,0,1:T(4,128)} %copy.10), calls=%async_computation | async-start | bytes 786432 | tf_op jit(solution)/shard_map/all_to_all | solution.py:243
  29.5 95.9 %all-reduce.5.cloned.1.call-start = ((), (), s32[]{:S(2)}) async-start(), calls=%async_computation.2 | async-start | bytes 6553600
  185.1 86.9 %copy-start.12 = (f32[2,768]{1,0:T(2,128)}, f32[2,768]{1,0:T(2,128)S(1)}, u32[]{:S(2)}) copy-start(f32[2,768]{1,0:T(2,128)S(1)} %add_divide_fusion) | copy-start | bytes 18436
Sparse Core Ops, SparseCore 0:
  32.7 72.5 all-reduce.4

commit v2 on v1

--- a/solution.py
+++ b/solution.py
@@ -247,7 +247,10 @@
         if k == 0:
             bottoms = totals[2:]
         star_means = (star_prior * star_ref + totals[:2]) / (star_prior + bottoms[k])
-        all_means = lax.all_gather(star_means, ("pix", "exp"), axis=1, tiled=False)
+        copies = jnp.broadcast_to(star_means[:, None, :], (2, peers, star_count))
+        all_means = lax.all_to_all(
+            copies, ("pix", "exp"), split_axis=1, concat_axis=1, tiled=True
+        )
         right = pl.pallas_call(
             functools.partial(right_kernel, peers),
             grid=(maps_device,),

time: 280 us -> 210 us (0.75)
  blocking collectives: 175 us -> 58.3 us
  waiting for transfers between devices: 12.2 us -> 56.1 us
    all_gather x2 -> x0, blocking collectives: 133 us -> none  [on_device(): all_means = lax.all_gather(star_means, ('pix', 'exp'), axis=1, tiled=False)]
    unnamed x2, waiting for transfers between devices: 0.68 us -> 36.1 us
    all_to_all x0 -> x1, blocking collectives: none -> 11.4 us  [on_device(): lax.all_to_all(copies, ('pix', 'exp'), split_axis=1, concat_axis=1, tiled...]
    all_to_all x0 -> x1, waiting for transfers between devices: none -> 7.25 us  [on_device(): lax.all_to_all(copies, ('pix', 'exp'), split_axis=1, concat_axis=1, tiled...]
    unnamed x2, blocking collectives: 20.2 us -> 23.4 us
    unnamed x35 -> x33, local copies, waits for them, and re-layouts: 7.87 us -> 7.85 us
  transfers between devices with their start and end apart: 2 -> 3, of which waited for: 1 -> 3; matrix products, arithmetic and copies ran while one was open for 1% -> 1% of each run, Pallas kernels for 2% -> 2%
where the time goes in v2:
time: 210 us; the launch traced here: 209 us
  blocking collectives  58.3 us (28%)
  Pallas kernels  57.2 us (27%)
  waiting for transfers between devices  56.1 us (27%)
  between operations  14.9 us (7%)
  starting transfers between devices  9.98 us (5%)
  local copies, waits for them, and re-layouts  9.89 us (5%)
    unnamed x2, waiting for transfers between devices  36.1 us
    pallas_call x1, Pallas kernels, invert(): pl.pallas_call(inverse_kernel, out_shape=jax.ShapeDtypeStruct((count, siz...  35.2 us
    unnamed x2, blocking collectives  23.4 us
    pallas_call x2, Pallas kernels, sums_call(): pl.pallas_call(functools.partial(sums_kernel, peers, chosen), out_shape=t...  13.5 us
    all_to_all x1, blocking collectives, on_device(): lax.all_to_all(sums, ('pix', 'exp'), split_axis=1, concat_axis=1, tiled=T...  13.2 us
    all_to_all x1, waiting for transfers between devices, on_device(): lax.all_to_all(sums, ('pix', 'exp'), split_axis=1, concat_axis=1, tiled=T...  12.8 us
    all_to_all x1, blocking collectives, on_device(): lax.all_to_all(copies, ('pix', 'exp'), split_axis=1, concat_axis=1, tiled...  11.4 us
    all_gather x2, blocking collectives, on_device(): coefficients = lax.all_gather(own_maps + update, 'pix', axis=0, tiled=True)  10.3 us
  transfers between devices with their start and end apart: 3, of which 3 were waited for; matrix products, arithmetic and copies ran while one was open for 1% of the time, Pallas kernels for 2%

profile of v2, /device:TPU:0, one launch (start us, length us, event | category | flops | bytes accessed | tf_op | source)
XLA Modules:
  0.0 208.8 jit_solution(13683712465685189958)
XLA Ops:
  7.2 0.0 copy-start
  7.2 1.7 copy-done
  8.9 0.8 copy-done.2
  9.7 0.7 copy-done.4
  10.4 0.7 copy-done.6
  11.1 0.7 copy-done.8
  11.9 0.7 copy-done.10
  12.6 8.4 %shard_map.95 = (f32[2,8,200,200]{3,2,1,0:T(8,128)}, f32[2,6144]{1,0:T(2,128)S(1)}, f32[4,32,768]{2,1,0:T(8,128)S(1)}) custom-call(bf16[200,6144]{1,0:T(8,128)(2,1)S(1)} %copy-done, f32[1,6144]{1,0:T(1,128)S(1)} %bitcast.8, s32[2,6144]{1,0:T(2,128)S(1)} %copy-done.2, s32[1,6144]{1,0:T(1,128)S(1)} %bitcast.12, s32[1,6144]{1,0:T(1,128)S(1)} %bitcast.16, ...), custom_call_target="tpu_custom_call" | custom-call | tf_op jit(solution)/shard_map/pallas_call | solution.py:226
  21.0 0.0 copy-start.1
  21.0 0.0 copy-start.5
  21.0 0.0 copy-start.7
  21.0 0.0 copy-start.9
  21.0 1.0 copy.10
  22.1 7.4 %all-to-all-start = ((f32[4,32,768]{2,0,1:T(4,128)}), f32[4,32,768]{2,0,1:T(4,128)S(1)}, u32[]{:S(2)}, u32[]{:S(2)}) async-start(f32[4,32,768]{2,0,1:T(4,128)} %copy.10), calls=%async_computation | async-start | bytes 786432 | tf_op jit(solution)/shard_map/all_to_all | solution.py:243
  29.4 0.0 all-reduce.5.cloned.1.call-start
  29.5 0.7 all-reduce.5.cloned.1.call-update
  30.2 12.8 %all-to-all-done = f32[4,32,768]{2,0,1:T(4,128)S(1)} async-done(((f32[4,32,768]{2,0,1:T(4,128)}), f32[4,32,768]{2,0,1:T(4,128)S(1)}, u32[]{:S(2)}, u32[]{:S(2)}) %all-to-all-start) | async-done | bytes 393248 | tf_op jit(solution)/shard_map/all_to_all | solution.py:243
  43.0 0.1 reduce_sum.18
  43.1 0.0 copy-done.11
  43.1 0.0 copy-done.13
  43.1 0.7 broadcast_in_dim.4
  43.9 2.6 %all-to-all-start.1 = ((f32[2,32,768]{2,0,1:T(2,128)}), f32[2,32,768]{2,0,1:T(2,128)S(1)}, u32[]{:S(2)}, u32[]{:S(2)}) async-start(f32[2,32,768]{2,0,1:T(2,128)} %broadcast_in_dim.4), calls=%async_computation.1 | async-start | bytes 393216 | tf_op jit(solution)/shard_map/all_to_all | solution.py:251
  46.5 0.0 copy-done.3
  46.5 0.0 copy-done.14
  46.5 0.6 dynamic-slice
  47.8 7.3 %all-to-all-done.1 = f32[2,32,768]{2,0,1:T(2,128)S(1)} async-done(((f32[2,32,768]{2,0,1:T(2,128)}), f32[2,32,768]{2,0,1:T(2,128)S(1)}, u32[]{:S(2)}, u32[]{:S(2)}) %all-to-all-start.1) | async-done | bytes 196640 | tf_op jit(solution)/shard_map/all_to_all | solution.py:251
  55.0 0.0 copy-done.1
  55.1 0.0 copy-done.5
  55.1 0.0 copy-done.7
  55.1 4.2 %shard_map.96 = f32[8,2,200]{2,1,0:T(2,128)S(1)} custom-call(bf16[200,6144]{1,0:T(8,128)(2,1)S(1)} %copy-done.1, f32[1,6144]{1,0:T(1,128)S(1)} %bitcast.9, s32[1,6144]{1,0:T(1,128)S(1)} %get-tuple-element.14.mask_ref, s32[1,6144]{1,0:T(1,128)S(1)} %bitcast.13, s32[1,6144]{1,0:T(1,128)S(1)} %bitcast.17, f32[2,6144]{1,0:T(2,128)S(1)} %get-tuple-element.7.predicted_ref, ...), custom_call_target="tpu_custom_call" | custom-call | tf_op jit(solution)/shard_map/pallas_call | solution.py:254
  59.3 12.1 %all-reduce = f32[8,2,200]{2,1,0:T(2,128)S(1)} all-reduce(f32[8,2,200]{2,1,0:T(2,128)S(1)} %shard_map.96), channel_id=2, replica_groups=mesh['pix'=4,'exp'=8] {'pix'}, use_global_device_ids=true, to_apply=%region_1.0.clone | all-reduce | flops 3200 | bytes 25600
  71.5 35.4 %all-reduce.5.cloned.1.call-done = f32[2,8,200,200]{3,2,1,0:T(8,128)} async-done(((f32[2,8,200,200]{3,2,1,0:T(8,128)}), f32[2,8,200,200]{3,2,1,0:T(8,128)}) %all-reduce.5.cloned.1.call-update) | async-done | bytes 2560016
  106.9 1.2 constant_dynamic-slice_fusion
  108.1 35.2 %shard_map.97 = f32[4,200,200]{2,1,0:T(8,128)S(1)} custom-call(f32[4,200,200]{2,1,0:T(8,128)S(1)} %bitcast.7), custom_call_target="tpu_custom_call" | custom-call | tf_op jit(solution)/shard_map/pallas_call | solution.py:182
  143.2 1.0 convolution_add_fusion.1
  144.2 5.2 %all_gather.6.coef_ref = f32[8,2,200]{2,1,0:T(2,128)S(1)} all-gather(f32[2,2,200]{2,1,0:T(2,128)S(1)} %convolution_add_fusion.1), channel_id=1, replica_groups=mesh['pix'=4,'exp'=8] {'pix'}, dimensions={0}, use_global_device_ids=true | all-gather | bytes 16000 | tf_op jit(solution)/shard_map/all_gather | solution.py:271
  149.4 5.1 %shard_map.98 = (f32[2,6144]{1,0:T(2,128)S(1)}, f32[2,32,768]{2,1,0:T(8,128)S(1)}) custom-call(bf16[200,6144]{1,0:T(8,128)(2,1)S(1)} %copy-done.1, f32[1,6144]{1,0:T(1,128)S(1)} %bitcast.10, s32[2,6144]{1,0:T(2,128)S(1)} %copy-done.3, s32[1,6144]{1,0:T(1,128)S(1)} %bitcast.14, s32[1,6144]{1,0:T(1,128)S(1)} %bitcast.18, f32[8,2,200]{2,1,0:T(2,128)S(1)} %all_gather.6.coef_ref), custom_call_target="tpu_custom_call" | custom-call | tf_op jit(solution)/shard_map/pallas_call | solution.py:226
  154.5 0.2 copy.12
  154.7 13.2 %all_to_all.20 = f32[2,32,768]{2,0,1:T(2,128)} all-to-all(f32[2,32,768]{2,0,1:T(2,128)S(1)} %copy.12), channel_id=1, replica_groups=mesh['pix'=4,'exp'=8] {'pix','exp'}, dimensions={1} | all-to-all | bytes 393216 | tf_op jit(solution)/shard_map/all_to_all | solution.py:243
  167.9 1.0 reduce_sum.19
  168.9 0.0 copy-start.12
  168.9 0.1 broadcast_in_dim.5
  169.0 11.4 %all_to_all.21 = f32[2,32,768]{2,0,1:T(2,128)S(1)} all-to-all(f32[2,32,768]{2,0,1:T(2,128)S(1)} %broadcast_in_dim.5), channel_id=1, replica_groups=mesh['pix'=4,'exp'=8] {'pix','exp'}, dimensions={1} | all-to-all | bytes 393216 | tf_op jit(solution)/shard_map/all_to_all | solution.py:251
  180.4 4.2 %shard_map.99 = f32[8,2,200]{2,1,0:T(2,128)S(1)} custom-call(bf16[200,6144]{1,0:T(8,128)(2,1)S(1)} %copy-done.1, f32[1,6144]{1,0:T(1,128)S(1)} %bitcast.11, s32[1,6144]{1,0:T(1,128)S(1)} %get-tuple-element.15.mask_ref, s32[1,6144]{1,0:T(1,128)S(1)} %bitcast.15, s32[1,6144]{1,0:T(1,128)S(1)} %bitcast.19, f32[2,6144]{1,0:T(2,128)S(1)} %get-tuple-element.10.predicted_ref, ...), custom_call_target="tpu_custom_call" | custom-call | tf_op jit(solution)/shard_map/pallas_call | solution.py:254
  184.6 11.2 %all-reduce.2 = f32[8,2,200]{2,1,0:T(2,128)S(1)} all-reduce(f32[8,2,200]{2,1,0:T(2,128)S(1)} %shard_map.99), channel_id=4, replica_groups=mesh['pix'=4,'exp'=8] {'pix'}, use_global_device_ids=true, to_apply=%region_4.0.clone | all-reduce | flops 3200 | bytes 25600
  195.8 0.3 convolution_add_fusion
  196.2 5.2 %all_gather.7 = f32[8,2,200]{2,1,0:T(2,128)S(1)} all-gather(f32[2,2,200]{2,1,0:T(2,128)S(1)} %convolution_add_fusion), channel_id=1, replica_groups=mesh['pix'=4,'exp'=8] {'pix'}, dimensions={0}, use_global_device_ids=true | all-gather | bytes 16000 | tf_op jit(solution)/shard_map/all_gather | solution.py:271
  201.3 0.6 copy.18
  (18 shorter events, 0.1 us)
Async XLA Ops:
  7.2 1.7 copy-start
  8.9 0.8 copy-start.2
  9.7 0.7 copy-start.4
  10.4 0.7 copy-start.6
  11.1 0.7 copy-start.8
  11.9 0.7 copy-start.10
  21.0 22.1 %copy-start.11 = (f32[768]{0:T(1024)S(1)}, f32[768]{0:T(1024)}, u32[]{:S(2)}) copy-start(f32[768]{0:T(1024)} %param.15) | copy-start | bytes 9220
  21.0 22.1 %copy-start.13 = (f32[2,768]{1,0:T(2,128)S(1)}, f32[2,768]{1,0:T(2,128)}, u32[]{:S(2)}) copy-start(f32[2,768]{1,0:T(2,128)} %param.14) | copy-start | bytes 18436
  21.0 25.5 %copy-start.3 = (s32[2,6144]{1,0:T(2,128)S(1)}, s32[2,6144]{1,0:T(2,128)}, u32[]{:S(2)}) copy-start(s32[2,6144]{1,0:T(2,128)} %mask_ref.3) | copy-start | bytes 147460
  21.0 25.5 %copy-start.14 = (u32[32]{0:T(128)S(1)}, u32[32]{0:T(128)}, u32[]{:S(2)}) copy-start(u32[32]{0:T(128)} %constant.15) | copy-start | bytes 388
  21.0 34.0 %copy-start.1 = (bf16[200,6144]{1,0:T(8,128)(2,1)S(1)}, bf16[200,6144]{1,0:T(8,128)(2,1)}, u32[]{:S(2)}) copy-start(bf16[200,6144]{1,0:T(8,128)(2,1)} %design_ref.7) | copy-start | bytes 7372804
  21.0 34.0 %copy-start.5 = (f32[6144]{0:T(1024)S(1)}, f32[6144]{0:T(1024)}, u32[]{:S(2)}) copy-start(f32[6144]{0:T(1024)} %param.9) | copy-start | bytes 73732
  21.0 34.0 %copy-start.7 = (s32[6144,1]{0,1:T(1,128)S(1)}, s32[6144,1]{0,1:T(1,128)}, u32[]{:S(2)}) copy-start(s32[6144,1]{0,1:T(1,128)} %param.11) | copy-start | bytes 73732
  21.0 34.0 %copy-start.9 = (s32[6144]{0:T(1024)S(1)}, s32[6144]{0:T(1024)}, u32[]{:S(2)}) copy-start(s32[6144]{0:T(1024)} %param.12) | copy-start | bytes 73732
  22.1 20.9 %all-to-all-start = ((f32[4,32,768]{2,0,1:T(4,128)}), f32[4,32,768]{2,0,1:T(4,128)S(1)}, u32[]{:S(2)}, u32[]{:S(2)}) async-start(f32[4,32,768]{2,0,1:T(4,128)} %copy.10), calls=%async_computation | async-start | bytes 786432 | tf_op jit(solution)/shard_map/all_to_all | solution.py:243
  29.4 77.4 %all-reduce.5.cloned.1.call-start = ((), (), s32[]{:S(2)}) async-start(), calls=%async_computation.4 | async-start | bytes 6553600
  43.9 11.2 %all-to-all-start.1 = ((f32[2,32,768]{2,0,1:T(2,128)}), f32[2,32,768]{2,0,1:T(2,128)S(1)}, u32[]{:S(2)}, u32[]{:S(2)}) async-start(f32[2,32,768]{2,0,1:T(2,128)} %broadcast_in_dim.4), calls=%async_computation.1 | async-start | bytes 393216 | tf_op jit(solution)/shard_map/all_to_all | solution.py:251
  168.9 33.1 %copy-start.12 = (f32[2,768]{1,0:T(2,128)}, f32[2,768]{1,0:T(2,128)S(1)}, u32[]{:S(2)}) copy-start(f32[2,768]{1,0:T(2,128)S(1)} %add_divide_fusion) | copy-start | bytes 18436
Sparse Core Ops, SparseCore 0:
  32.6 74.1 all-reduce.4
